TPU v7x, 32 devices: a whole 2x2x4 slice. The times are simulated.
32 devices in a mesh: job: 2 (over x), fsdp: 8 (over z, y), replica: 2 (over core).
Axes of the slice: x: 2, y: 2, z: 4, core: 2. Of those that a mesh axis runs over, the one named last changes fastest.
Arguments:
- tokens: bfloat16 [4, 2, 1152, 2048], P(('job', 'replica'), None, 'fsdp'), parts along dimension 0, may hold values from -6 to 6
- queries: bfloat16 [4, 2, 1152, 2048], P(('job', 'replica'), None, 'fsdp'), parts along dimension 0, may hold values from -64 to 64
- targets: bfloat16 [4, 2, 1152, 2048], P(('job', 'replica'), None, 'fsdp'), parts along dimension 0, may hold values from -6 to 6
- gain: float32 [2048], replicated, may hold values from 0.5 to 1.5
- base: float32 [4096, 1024], P(('job', 'fsdp')), parts along dimension 0, may hold values from -4 to 4
- offset: float32 [2, 4096, 1024], P('replica', ('job', 'fsdp')), parts along dimension 1, may hold values from -3 to 3
- first_moment: float32 [2, 4096, 1024], P('replica', ('job', 'fsdp')), parts along dimension 1, may hold values from -0.0014648438 to 0.0014648438
- second_moment: float32 [2, 4096, 1024], P('replica', ('job', 'fsdp')), parts along dimension 1, may hold values from 1e-09 to 1e-06
- outer_momentum: float32 [4096, 1024], P(('job', 'fsdp')), parts along dimension 0, may hold values from -1.5 to 1.5
- exponents: int32 [4096, 8], P(('job', 'fsdp')), parts along dimension 0, may hold values from -12 to -6
Outputs:
- new_base: float32 [4096, 1024], P(('job', 'fsdp')), parts along dimension 0
- new_momentum: float32 [4096, 1024], P(('job', 'fsdp')), parts along dimension 0
There are 2 independent parts, one for each index of `job`. A program takes and returns all parts, laid end to end along the dimension named above; an argument that names none is the same for every part. Nothing has to cross between parts.
All inputs are finite; a program needn't handle non-finite values.
Results may differ from a plain program's by a relative error of at most 0.024.
Values may be sent and summed in bfloat16 or wider, within the bound.
A program may use at most 64 MiB of HBM per device.

v0:
```python
import jax
import jax.numpy as jnp
from jax import lax
from jax.sharding import PartitionSpec as P

D = 2048
HEADS = 32
KV_HEADS = 8
HEAD = 64


def normalize(hidden, gain):
    values = hidden.astype(jnp.float32)
    power = jnp.mean(values * values, axis=-1, keepdims=True)
    return (values * lax.rsqrt(power + 1e-05) * gain).astype(jnp.bfloat16)


def sequence_grad(query, keyval, target, tok_total):
    length = query.shape[0]
    group = HEADS // KV_HEADS
    width = KV_HEADS * HEAD
    scale = HEAD ** (-0.5)
    qh = query.reshape(length, KV_HEADS, group, HEAD)
    keys = keyval[:, :width].reshape(length, KV_HEADS, HEAD)
    values = keyval[:, width:].reshape(length, KV_HEADS, HEAD)
    scores = jnp.einsum("qhgd,khd->hgqk", qh, keys, preferred_element_type=jnp.float32) * scale
    causal = jnp.arange(length)[:, None] >= jnp.arange(length)[None, :]
    scores = jnp.where(causal, scores, -1e30)
    top = jnp.max(scores, axis=-1, keepdims=True)
    expo = jnp.exp(scores - top)
    probs = expo / jnp.sum(expo, axis=-1, keepdims=True)
    probs_b = probs.astype(jnp.bfloat16)
    output = jnp.einsum("hgqk,khd->qhgd", probs_b, values, preferred_element_type=jnp.float32)
    goal = target.reshape(length, KV_HEADS, group, HEAD).astype(jnp.float32)
    grad_out = ((output - goal) / tok_total).astype(jnp.bfloat16)
    grad_v = jnp.einsum("hgqk,qhgd->khd", probs_b, grad_out, preferred_element_type=jnp.float32)
    grad_p = jnp.einsum("qhgd,khd->hgqk", grad_out, values, preferred_element_type=jnp.float32)
    grad_s = probs * (grad_p - jnp.sum(probs * grad_p, axis=-1, keepdims=True))
    grad_sb = (grad_s * scale).astype(jnp.bfloat16)
    grad_k = jnp.einsum("hgqk,qhgd->khd", grad_sb, qh, preferred_element_type=jnp.float32)
    joined = jnp.concatenate([grad_k.reshape(length, width), grad_v.reshape(length, width)], axis=1)
    return (joined * D ** (-0.5)).astype(jnp.bfloat16)


def adam_update(weights, mom1, mom2, grad):
    mom1 = 0.9 * mom1 + 0.1 * grad
    mom2 = 0.95 * mom2 + 0.05 * grad * grad
    weights = weights - 0.08 * (mom1 / (jnp.sqrt(mom2) + 1e-08) + 0.01 * weights)
    return (weights, mom1, mom2)


def shards(
    tokens,
    queries,
    targets,
    gain,
    base,
    offset,
    first_moment,
    second_moment,
    outer_momentum,
    exponents,
):
    rows = base.shape[0]
    tok_local = tokens.shape[2]
    members = lax.axis_size("fsdp")
    tok_total = tok_local * members
    weights = base + offset[0]
    mom1 = first_moment[0]
    mom2 = second_moment[0]
    for step in range(tokens.shape[1]):
        normed = normalize(tokens[0, step], gain)
        wide = weights.astype(jnp.bfloat16)
        whole = lax.all_gather(wide, "fsdp", axis=0, tiled=True)
        projected = jnp.dot(normed, whole, preferred_element_type=jnp.float32)
        keyval = (projected * D ** (-0.5)).astype(jnp.bfloat16)
        grad_kv = sequence_grad(queries[0, step], keyval, targets[0, step], tok_total)
        columns = lax.all_to_all(normed, "fsdp", split_axis=1, concat_axis=0, tiled=True)
        gathered = lax.all_gather(grad_kv, "fsdp", axis=0, tiled=True)
        seq_cols = columns.reshape(members, tok_local, rows)
        seq_grads = gathered.reshape(members, tok_local, grad_kv.shape[1])
        parts = jnp.einsum("ntr,ntc->nrc", seq_cols, seq_grads, preferred_element_type=jnp.float32)
        grad = jnp.sum(parts.astype(jnp.bfloat16).astype(jnp.float32), axis=0)
        weights, mom1, mom2 = adam_update(weights, mom1, mom2, grad)
    blocks = exponents.shape[1]
    block_len = base.shape[1] // blocks
    scale = jnp.exp2(exponents.astype(jnp.float32))[:, :, None]
    delta = (base - weights).reshape(rows, blocks, block_len)
    coded = jnp.clip(delta / scale, -448.0, 448.0).astype(jnp.bfloat16)
    replicas = lax.axis_size("replica")
    total = lax.psum(coded.astype(jnp.float32).astype(jnp.bfloat16), "replica").astype(jnp.float32)
    average = (total * scale / replicas).reshape(rows, blocks * block_len)
    new_momentum = 0.9 * outer_momentum + average
    new_base = base - 0.7 * (0.9 * new_momentum + average)
    return (new_base, new_momentum)


def solution(mesh):
    in_specs = (
        P(("job", "replica"), None, "fsdp", None),
        P(("job", "replica"), None, "fsdp", None),
        P(("job", "replica"), None, "fsdp", None),
        P(),
        P(("job", "fsdp"), None),
        P("replica", ("job", "fsdp"), None),
        P("replica", ("job", "fsdp"), None),
        P("replica", ("job", "fsdp"), None),
        P(("job", "fsdp"), None),
        P(("job", "fsdp"), None),
    )
    out_specs = (P(("job", "fsdp"), None), P(("job", "fsdp"), None))
    return jax.shard_map(shards, mesh=mesh, in_specs=in_specs, out_specs=out_specs, check_vma=False)
```

profile of v0, /device:TPU:0, one launch (start us, length us, event | category | flops | bytes accessed | tf_op | source)
XLA Modules:
  0.0 375.9 jit_solution(1945820226877589736)
XLA Ops:
  7.2 0.0 all-gather.5.cloned.1.call-start
  7.2 2.5 fusion.74
  9.7 0.0 all-gather.5.cloned.1.call-update
  9.7 0.0 all-gather.7.cloned.1.call-start
  9.8 2.2 fusion.90
  11.9 1.3 copy.34
  13.2 1.5 slice_convert_fusion.1
  14.7 1.8 copy.38
  16.6 0.6 iota_compare_fusion
  17.2 1.6 fusion.32
  18.8 68.1 %all-gather.5.cloned.1.call-done = bf16[2048,1024]{1,0:T(8,128)(2,1)} async-done(((bf16[256,1024]{1,0:T(8,128)(2,1)}), bf16[2048,1024]{1,0:T(8,128)(2,1)}) %all-gather.5.cloned.1.call-update) | async-done | bytes 4194320 | tf_op jit(solution)/shard_map/all_gather | solution.py:74
  86.8 3.2 fusion.30
  90.1 0.8 copy.72
  90.9 0.2 reshape.112
  91.1 0.2 copy.59
  91.4 5.9 %fusion.93 = (f32[8,4,144]{2,1,0:T(4,128)}, f32[8,4,144,144]{2,3,1,0:T(8,128)}) fusion(pred[144,144]{0,1:T(8,128)(4,1)} %iota_compare_fusion, bf16[144,8,64,1]{0,2,3,1:T(8,128)(2,1)} %bitcast.227, bf16[144,8,4,64]{0,3,2,1:T(8,128)(2,1)} %bitcast.218), kind=kOutput, calls=%fused_computation.128 | convolution fusion | flops 87589008 | bytes 3430656 | tf_op jit(solution)/shard_map/sub | solution.py:30
  97.2 3.0 fusion.27
  100.3 3.1 fusion.95
  103.4 0.6 copy-done.16
  104.0 1.7 fusion.45
  105.7 8.4 %fusion.12 = f32[8,144,64,1]{1,2,3,0:T(8,128)S(1)} fusion(bf16[144,8,4,64]{0,3,2,1:T(8,128)(2,1)} %bitcast.219, f32[8,144,144,4]{2,1,3,0:T(8,128)} %fusion.95, f32[8,4,144,144]{2,3,1,0:T(8,128)} %get-tuple-element.19, f32[8,4,144]{2,1,0:T(4,128)S(1)} %copy-done.17), kind=kOutput, calls=%fused_computation.22 | convolution fusion | flops 89584272 | bytes 6211584 | tf_op jit(solution)/shard_map/hgqk,qhgd->khd/dot_general | solution.py:40
  114.2 0.2 copy.77
  114.3 1.2 copy.78
  115.5 0.8 fusion.64
  116.3 0.0 all-gather.7.cloned.1.call-update
  116.3 0.0 all-gather.9.cloned.1.call-start
  116.4 0.3 slice_convert_fusion.2
  116.7 0.4 copy.86
  117.1 0.4 copy.87
  117.5 1.7 fusion.39
  119.3 29.1 %all_to_all.26 = bf16[144,8,256]{2,0,1:T(8,128)(2,1)} all-to-all(bf16[144,8,256]{2,0,1:T(8,128)(2,1)S(1)} %get-tuple-element.17), channel_id=1, replica_groups=mesh['job'=2,'fsdp'=8,'replica'=2] {'fsdp'}, dimensions={1} | all-to-all | bytes 1179648 | tf_op jit(solution)/shard_map/all_to_all | solution.py:78
  148.3 27.5 %all-gather.7.cloned.1.call-done = bf16[1152,1024]{1,0:T(8,128)(2,1)} async-done(((bf16[144,1024]{1,0:T(8,128)(2,1)}), bf16[1152,1024]{1,0:T(8,128)(2,1)}) %all-gather.7.cloned.1.call-update) | async-done | bytes 2359312 | tf_op jit(solution)/shard_map/all_gather | solution.py:79
  175.8 3.3 convert_reduce_fusion.1
  179.2 1.0 copy-done.7
  180.2 1.6 fusion.89
  181.8 0.0 all-gather.11.cloned.1.call-start
  181.8 2.2 copy.45
  184.0 1.8 copy.49
  185.8 68.0 %all-gather.9.cloned.1.call-done = bf16[2048,1024]{1,0:T(8,128)(2,1)} async-done(((bf16[256,1024]{1,0:T(8,128)(2,1)}), bf16[2048,1024]{1,0:T(8,128)(2,1)}) %all-gather.9.cloned.1.call-update) | async-done | bytes 4194320 | tf_op jit(solution)/shard_map/all_gather | solution.py:74
  253.9 3.2 fusion.31
  257.1 0.1 copy.79
  257.2 0.2 reshape.117
  257.4 0.2 copy.67
  257.7 5.1 %fusion.94 = (f32[8,4,144]{2,1,0:T(4,128)S(1)}, f32[8,4,144,144]{2,3,1,0:T(8,128)}) fusion(pred[144,144]{0,1:T(8,128)(4,1)S(1)} %copy-done.12, bf16[144,8,64,1]{0,2,3,1:T(8,128)(2,1)S(1)} %bitcast.226, bf16[144,8,4,64]{0,3,2,1:T(8,128)(2,1)} %bitcast.220), kind=kOutput, calls=%fused_computation.129 | convolution fusion | flops 87589008 | bytes 3430656 | tf_op jit(solution)/shard_map/sub | solution.py:30
  262.8 3.7 fusion.25
  266.5 3.1 fusion.96
  269.5 0.7 copy-done.15
  270.2 1.7 fusion.42
  272.0 8.2 %fusion.14 = f32[8,144,64,1]{1,2,3,0:T(8,128)} fusion(bf16[144,8,4,64]{0,3,2,1:T(8,128)(2,1)S(1)} %bitcast.221, f32[8,144,144,4]{2,1,3,0:T(8,128)} %fusion.96, f32[8,4,144,144]{2,3,1,0:T(8,128)} %get-tuple-element.21, f32[8,4,144]{2,1,0:T(4,128)S(1)} %get-tuple-element.20), kind=kOutput, calls=%fused_computation.23 | convolution fusion | flops 89584272 | bytes 6211584 | tf_op jit(solution)/shard_map/hgqk,qhgd->khd/dot_general | solution.py:40
  280.2 1.2 copy.84
  281.4 1.9 copy.85
  283.3 1.8 fusion.65
  285.1 4.2 %all-to-all-start.1 = ((bf16[144,8,256]{2,0,1:T(8,128)(2,1)}), bf16[144,8,256]{2,0,1:T(8,128)(2,1)}, u32[]{:S(2)}, u32[]{:S(2)}) async-start(bf16[144,8,256]{2,0,1:T(8,128)(2,1)} %get-tuple-element.16), calls=%async_computation.1 | async-start | bytes 1179648 | tf_op jit(solution)/shard_map/all_to_all | solution.py:78
  289.4 0.3 all-reduce.2.cloned.1.call-start
  289.7 0.1 copy.55
  289.8 24.1 %all-to-all-done.1 = bf16[144,8,256]{2,0,1:T(8,128)(2,1)} async-done(((bf16[144,8,256]{2,0,1:T(8,128)(2,1)}), bf16[144,8,256]{2,0,1:T(8,128)(2,1)}, u32[]{:S(2)}, u32[]{:S(2)}) %all-to-all-start.1) | async-done | bytes 589856 | tf_op jit(solution)/shard_map/all_to_all | solution.py:78
  313.9 28.6 %all-gather.11.cloned.1.call-done = bf16[1152,1024]{1,0:T(8,128)(2,1)} async-done(((bf16[144,1024]{1,0:T(8,128)(2,1)}), bf16[1152,1024]{1,0:T(8,128)(2,1)}) %all-gather.11.cloned.1.call-update) | async-done | bytes 2359312 | tf_op jit(solution)/shard_map/all_gather | solution.py:79
  342.5 3.3 convert_reduce_fusion
  345.9 1.5 fusion.61
  347.4 0.2 copy.88
  347.6 1.1 fusion.60
  348.8 17.4 %all-reduce.2.cloned.1.call-done = bf16[256,8,128]{2,1,0:T(8,128)(2,1)} async-done(((bf16[256,8,128]{2,1,0:T(8,128)(2,1)}), bf16[256,8,128]{2,1,0:T(8,128)(2,1)}) %all-reduce.2.cloned.1.call-update) | async-done | bytes 524304 | tf_op jit(solution)/shard_map/psum | solution.py:91
  366.2 1.4 multiply_multiply_fusion.2
  367.6 1.8 fusion.58
  (42 shorter events, 0.2 us)
Async XLA Ops:
  7.2 79.7 %all-gather.5.cloned.1.call-start = ((), (), s32[]{:S(2)}) async-start(), calls=%async_computation.2 | async-start | bytes 4718592 | tf_op jit(solution)/shard_map/all_gather | solution.py:74
  9.7 166.1 %all-gather.7.cloned.1.call-start = ((), (), s32[]{:S(2)}) async-start(), calls=%async_computation.3 | async-start | bytes 2654208 | tf_op jit(solution)/shard_map/all_gather | solution.py:79
  13.2 73.6 %copy-start.13 = (f32[2048]{0:T(1024)S(1)}, f32[2048]{0:T(1024)}, u32[]{:S(2)}) copy-start(f32[2048]{0:T(1024)} %param.13) | copy-start | bytes 24580
  91.4 5.9 %copy-start.9 = (f32[1,1,144,2048]{2,3,1,0:T(8,128)S(1)}, f32[1,1,144,2048]{2,3,1,0:T(8,128)}, u32[]{:S(2)}) copy-start(f32[1,1,144,2048]{2,3,1,0:T(8,128)} %copy.38) | copy-start | bytes 3538948
  100.2 3.8 copy-start.16
  100.3 3.8 copy-start.17
  105.7 10.7 %copy-start.2 = (bf16[1,2,144,2048]{3,2,1,0:T(8,128)(2,1)S(1)}, bf16[1,2,144,2048]{3,2,1,0:T(8,128)(2,1)}, u32[]{:S(2)}) copy-start(bf16[1,2,144,2048]{3,2,1,0:T(8,128)(2,1)} %param.10) | copy-start | bytes 3538948
  116.3 137.5 %all-gather.9.cloned.1.call-start = ((), (), s32[]{:S(2)}) async-start(), calls=%async_computation.4 | async-start | bytes 4718592 | tf_op jit(solution)/shard_map/all_gather | solution.py:74
  119.3 60.9 %copy-start = (f32[256,1024]{1,0:T(8,128)S(1)}, f32[256,1024]{1,0:T(8,128)}, u32[]{:S(2)}) copy-start(f32[256,1024]{1,0:T(8,128)} %param.14) | copy-start | bytes 3145732
  119.3 60.9 %copy-start.1 = (f32[1,256,1024]{2,1,0:T(8,128)S(1)}, f32[1,256,1024]{2,1,0:T(8,128)}, u32[]{:S(2)}) copy-start(f32[1,256,1024]{2,1,0:T(8,128)} %param.15) | copy-start | bytes 3145732
  175.8 4.3 %copy-start.3 = (f32[1,256,1024]{2,1,0:T(8,128)S(1)}, f32[1,256,1024]{2,1,0:T(8,128)}, u32[]{:S(2)}) copy-start(f32[1,256,1024]{2,1,0:T(8,128)} %param.17) | copy-start | bytes 3145732
  175.8 4.3 %copy-start.5 = (f32[1,256,1024]{2,1,0:T(8,128)S(1)}, f32[1,256,1024]{2,1,0:T(8,128)}, u32[]{:S(2)}) copy-start(f32[1,256,1024]{2,1,0:T(8,128)} %param.16) | copy-start | bytes 3145732
  179.2 1.0 copy-start.7
  181.8 160.7 %all-gather.11.cloned.1.call-start = ((), (), s32[]{:S(2)}) async-start(), calls=%async_computation.5 | async-start | bytes 2654208 | tf_op jit(solution)/shard_map/all_gather | solution.py:79
  185.8 71.9 %copy-start.12 = (pred[144,144]{0,1:T(8,128)(4,1)S(1)}, pred[144,144]{0,1:T(8,128)(4,1)}, u32[]{:S(2)}) copy-start(pred[144,144]{0,1:T(8,128)(4,1)} %iota_compare_fusion) | copy-start | bytes 62212
  266.4 3.8 %copy-start.15 = (f32[8,4,144,144]{2,3,1,0:T(8,128)S(1)}, f32[8,4,144,144]{2,3,1,0:T(8,128)}, u32[]{:S(2)}) copy-start(f32[8,4,144,144]{2,3,1,0:T(8,128)} %get-tuple-element.21) | copy-start | bytes 7962628
  270.2 1.7 copy-start.11
  272.0 17.7 %copy-start.14 = (s32[256,8]{0,1:T(8,128)S(1)}, s32[256,8]{0,1:T(8,128)}, u32[]{:S(2)}) copy-start(s32[256,8]{0,1:T(8,128)} %param.19) | copy-start | bytes 24580
  283.3 62.6 %copy-start.4 = (f32[1,256,1024]{2,1,0:T(8,128)S(1)}, f32[1,256,1024]{2,1,0:T(8,128)}, u32[]{:S(2)}) copy-start(f32[1,256,1024]{2,1,0:T(8,128)} %param.17) | copy-start | bytes 3145732
  285.1 28.7 %all-to-all-start.1 = ((bf16[144,8,256]{2,0,1:T(8,128)(2,1)}), bf16[144,8,256]{2,0,1:T(8,128)(2,1)}, u32[]{:S(2)}, u32[]{:S(2)}) async-start(bf16[144,8,256]{2,0,1:T(8,128)(2,1)} %get-tuple-element.16), calls=%async_computation.1 | async-start | bytes 1179648 | tf_op jit(solution)/shard_map/all_to_all | solution.py:78
  289.4 76.8 %all-reduce.2.cloned.1.call-start = ((), (), s32[]{:S(2)}) async-start(), calls=%async_computation.6 | async-start | bytes 1048576 | tf_op jit(solution)/shard_map/psum | solution.py:91
  342.5 3.4 copy-start.6
  342.5 3.4 copy-start.8
  347.4 20.2 %copy-start.10 = (f32[256,1024]{1,0:T(8,128)S(1)}, f32[256,1024]{1,0:T(8,128)}, u32[]{:S(2)}) copy-start(f32[256,1024]{1,0:T(8,128)} %param.18) | copy-start | bytes 3145732
Sparse Core Ops, SparseCore 0:
  10.7 76.0 all-gather.4
  116.5 59.3 all-gather.6
  181.9 71.9 all-gather.8
  285.3 57.1 all-gather.10
  348.9 17.2 all-reduce.1
where the time goes:
time: 377 us; the launch traced here: 376 us
  waiting for transfers between devices  234 us (62%)
  matrix products  57 us (15%)
  blocking collectives  29.1 us (8%)
  local copies, waits for them, and re-layouts  19.1 us (5%)
  other arithmetic  18.2 us (5%)
  between operations  14.1 us (4%)
  starting transfers between devices  4.63 us (1%)
    all_gather x2, waiting for transfers between devices, shards(): whole = lax.all_gather(wide, 'fsdp', axis=0, tiled=True)  136 us
    all_gather x2, waiting for transfers between devices, shards(): gathered = lax.all_gather(grad_kv, 'fsdp', axis=0, tiled=True)  56.1 us
    all_to_all x1, blocking collectives, shards(): lax.all_to_all(normed, 'fsdp', split_axis=1, concat_axis=0, tiled=True)  29.1 us
    all_to_all x1, waiting for transfers between devices, shards(): lax.all_to_all(normed, 'fsdp', split_axis=1, concat_axis=0, tiled=True)  24.1 us
    psum x1, waiting for transfers between devices, shards(): lax.psum(coded.astype(jnp.float32).astype(jnp.bfloat16), 'replica')  17.4 us
    dot_general x2, matrix products, sequence_grad(): jnp.einsum('hgqk,qhgd->khd', grad_sb, qh, preferred_element_type=jnp.floa...  16.6 us
    sub x2, matrix products, sequence_grad(): expo = jnp.exp(scores - top)  11 us
  transfers between devices with their start and end apart: 6, of which 6 were waited for; matrix products, arithmetic and copies ran while one was open for 4% of the time, Pallas kernels for 0%

commit v1 on v0

v1 whole, which is shorter than its diff:
```python
import functools

import jax
import jax.numpy as jnp
from jax import lax
from jax.experimental import pallas as pl
from jax.experimental.pallas import tpu as pltpu
from jax.sharding import PartitionSpec as P

D = 2048
HEADS = 32
KV_HEADS = 8
HEAD = 64
CHUNKS = 4
GROUP = HEADS // KV_HEADS
KVD = KV_HEADS * HEAD
HALF = KVD // CHUNKS
WIDE = 2 * HALF
MESH = pl.DeviceIdType.MESH


def ring_device(place, n):
    place = lax.rem(place + 2 * n, n)
    if n != 8:
        return place
    return jnp.where(place < n // 2, 2 * place, 2 * n - 1 - 2 * place)


def ring_place(device, n):
    if n != 8:
        return device
    return jnp.where(lax.rem(device, 2) == 0, device // 2, n - 1 - device // 2)


def columns(c, half):
    return slice(half * KVD + c * HALF, half * KVD + (c + 1) * HALF)


def head_grads(qs, ts, kv, tok_total):
    length = kv.shape[0]
    keys, vals = [], []
    row = lax.broadcasted_iota(jnp.int32, (length, length), 0)
    col = lax.broadcasted_iota(jnp.int32, (length, length), 1)
    causal = jnp.concatenate([row >= col] * GROUP, axis=0)
    nt = (((1,), (1,)), ((), ()))
    tn = (((0,), (0,)), ((), ()))
    for j in range(HALF // HEAD):
        k = kv[:, j * HEAD : (j + 1) * HEAD]
        v = kv[:, HALF + j * HEAD : HALF + (j + 1) * HEAD]
        heads = [slice((j * GROUP + i) * HEAD, (j * GROUP + i + 1) * HEAD) for i in range(GROUP)]
        q = jnp.concatenate([qs[:, h] for h in heads], axis=0)
        goal = jnp.concatenate([ts[:, h] for h in heads], axis=0).astype(jnp.float32)
        scores = lax.dot_general(q, k, nt, preferred_element_type=jnp.float32) * HEAD ** (-0.5)
        scores = jnp.where(causal, scores, -1e30)
        top = jnp.max(scores, axis=-1, keepdims=True)
        expo = jnp.exp(scores - top)
        probs = expo * (1.0 / jnp.sum(expo, axis=-1, keepdims=True))
        probs_b = probs.astype(jnp.bfloat16)
        out = jnp.dot(probs_b, v, preferred_element_type=jnp.float32)
        grad_out = ((out - goal) * (1.0 / tok_total)).astype(jnp.bfloat16)
        grad_v = lax.dot_general(probs_b, grad_out, tn, preferred_element_type=jnp.float32)
        grad_p = lax.dot_general(grad_out, v, nt, preferred_element_type=jnp.float32)
        inner = jnp.sum(probs * grad_p, axis=-1, keepdims=True)
        grad_sb = (probs * (grad_p - inner) * HEAD ** (-0.5)).astype(jnp.bfloat16)
        grad_k = lax.dot_general(grad_sb, q, tn, preferred_element_type=jnp.float32)
        keys.append(grad_k)
        vals.append(grad_v)
    joined = jnp.concatenate(keys + vals, axis=1)
    return (joined * D ** (-0.5)).astype(jnp.bfloat16)


def kernel(
    n, tok_total,
    tok_ref, gain_ref, base_ref, off_ref, inv_ref, q_hbm, t_hbm, m_hbm, v_hbm,
    out_ref,
    q_ref, t_ref, m_ref, v_ref, w_ref, wall, gall, nsend, cols, kvacc, gacc, coded,
    load_sem, w_send, w_recv, g_send, g_recv, a_send, a_recv, c_send, c_recv,
):
    me = lax.axis_index("fsdp")
    rep = lax.axis_index("replica")
    place = ring_place(me, n)
    near = (ring_device(place + 1, n), ring_device(place - 1, n))
    steps = tok_ref.shape[0]
    rows = base_ref.shape[0]
    last = n // 2

    barrier = pltpu.get_barrier_semaphore()
    for k in range(1, n):
        pl.semaphore_signal(barrier, inc=1, device_id={"fsdp": lax.rem(me + k, n)}, device_id_type=MESH)
    pl.semaphore_signal(barrier, inc=1, device_id={"replica": 1 - rep}, device_id_type=MESH)

    loads = [
        pltpu.make_async_copy(src, dst, load_sem.at[i])
        for i, (src, dst) in enumerate(((q_hbm, q_ref), (t_hbm, t_ref), (m_hbm, m_ref), (v_hbm, v_ref)))
    ]
    for load in loads:
        load.start()

    def put_wide(s, c, half, w):
        wall[s, me, c, :, half * HALF : (half + 1) * HALF] = w.astype(jnp.bfloat16)

    for c in range(CHUNKS):
        for half in (0, 1):
            w = base_ref[:, columns(c, half)] + off_ref[:, columns(c, half)]
            w_ref[:, columns(c, half)] = w
            put_wide(0, c, half, w)

    pl.semaphore_wait(barrier, n)

    sends = []

    def hop_copy(buf, send, recv, s, c, d, h, owner):
        return pltpu.make_async_remote_copy(
            src_ref=buf.at[s, owner, c], dst_ref=buf.at[s, owner, c],
            send_sem=send.at[s, c, d, h], recv_sem=recv.at[s, c, d, h],
            device_id={"fsdp": near[d]}, device_id_type=MESH,
        )

    def ring_start(ring, s, c):
        for d in (0, 1):
            copy = hop_copy(*ring, s, c, d, 0, me)
            copy.start()
            sends.append(copy)

    def ring_hop(ring, s, c, h):
        owners = []
        for d in (0, 1):
            if h == last and d != c % 2:
                continue
            owner = ring_device(place - h if d == 0 else place + h, n)
            hop_copy(*ring, s, c, d, h - 1, owner).wait_recv()
            if h < last - 1 or (h == last - 1 and d == c % 2):
                copy = hop_copy(*ring, s, c, d, h, owner)
                copy.start()
                sends.append(copy)
            owners.append(owner)
        return owners

    w_ring = (wall, w_send, w_recv)
    g_ring = (gall, g_send, g_recv)
    tn = (((0,), (0,)), ((), ()))

    for c in range(CHUNKS):
        ring_start(w_ring, 0, c)

    for s in range(steps):
        values = tok_ref[s].astype(jnp.float32)
        power = jnp.mean(values * values, axis=-1, keepdims=True)
        normed = (values * lax.rsqrt(power + 1e-05) * gain_ref[...]).astype(jnp.bfloat16)
        for p in range(n):
            nsend[s, p] = normed[:, p * rows : (p + 1) * rows]
        cols[s, me] = nsend[s, me]

    def swap_copy(s, k):
        to = lax.rem(me + k, n)
        return pltpu.make_async_remote_copy(
            src_ref=nsend.at[s, to], dst_ref=cols.at[s, me],
            send_sem=a_send.at[s, k], recv_sem=a_recv.at[s, k],
            device_id={"fsdp": to}, device_id_type=MESH,
        )

    def kv_add(s, c, owner, first=False):
        part = jnp.dot(nsend[s, owner], wall[s, owner, c], preferred_element_type=jnp.float32)
        kvacc[c] = part if first else kvacc[c] + part

    def grad_add(s, c, owner, first=False):
        part = lax.dot_general(cols[s, owner], gall[s, owner, c], tn, preferred_element_type=jnp.float32)
        part = part.astype(jnp.bfloat16).astype(jnp.float32)
        gacc[c] = part if first else gacc[c] + part

    def attend(s, c):
        kv = (kvacc[c] * D ** (-0.5)).astype(jnp.bfloat16)
        span = slice(c * GROUP * HALF, (c + 1) * GROUP * HALF)
        gall[s, me, c] = head_grads(q_ref[s, :, span], t_ref[s, :, span], kv, tok_total)

    def code_copy(c):
        return pltpu.make_async_remote_copy(
            src_ref=coded.at[0, c], dst_ref=coded.at[1, c],
            send_sem=c_send.at[c], recv_sem=c_recv.at[c],
            device_id={"replica": 1 - rep}, device_id_type=MESH,
        )

    def adam(s, c):
        for half in (0, 1):
            at = columns(c, half)
            inside = slice(half * HALF, (half + 1) * HALF)
            grad = gacc[c, :, inside]
            mom1 = 0.9 * m_ref[:, at] + 0.1 * grad
            mom2 = 0.95 * v_ref[:, at] + 0.05 * grad * grad
            w = w_ref[:, at]
            w = w - 0.08 * (mom1 / (jnp.sqrt(mom2) + 1e-08) + 0.01 * w)
            if s < steps - 1:
                m_ref[:, at] = mom1
                v_ref[:, at] = mom2
                w_ref[:, at] = w
                put_wide(s + 1, c, half, w)
            else:
                block = half * CHUNKS + c
                delta = (base_ref[:, at] - w) * inv_ref[:, block : block + 1]
                coded[0, c, :, inside] = jnp.clip(delta, -448.0, 448.0).astype(jnp.bfloat16)

    for s in range(steps):
        for c in range(CHUNKS):
            kv_add(s, c, me, True)
        for h in range(1, last + 1):
            for c in range(CHUNKS):
                for owner in ring_hop(w_ring, s, c, h):
                    kv_add(s, c, owner)
        for k in range(1, n):
            copy = swap_copy(s, k)
            copy.start()
            sends.append(copy)
        if s == 0:
            for load in loads:
                load.wait()
        for c in range(CHUNKS):
            attend(s, c)
            ring_start(g_ring, s, c)
        for c in range(CHUNKS):
            grad_add(s, c, me, True)
        for k in range(1, n):
            pltpu.make_async_remote_copy(
                src_ref=nsend.at[s, me], dst_ref=cols.at[s, lax.rem(me - k + n, n)],
                send_sem=a_send.at[s, k], recv_sem=a_recv.at[s, k],
                device_id={"fsdp": lax.rem(me + k, n)}, device_id_type=MESH,
            ).wait_recv()
        for h in range(1, last + 1):
            for c in range(CHUNKS):
                for owner in ring_hop(g_ring, s, c, h):
                    grad_add(s, c, owner)
        for c in range(CHUNKS):
            adam(s, c)
            if s < steps - 1:
                ring_start(w_ring, s + 1, c)
            else:
                copy = code_copy(c)
                copy.start()
                sends.append(copy)
    for c in range(CHUNKS):
        code_copy(c).wait_recv()
        for half in (0, 1):
            inside = slice(half * HALF, (half + 1) * HALF)
            out_ref[:, columns(c, half)] = (
                coded[0, c, :, inside].astype(jnp.float32) + coded[1, c, :, inside].astype(jnp.float32)
            )
    for copy in sends:
        copy.wait_send()


def shards(
    n, replicas,
    tokens, queries, targets, gain, base, offset,
    first_moment, second_moment, outer_momentum, exponents,
):
    rows, width = base.shape
    steps, length = tokens.shape[1], tokens.shape[2]
    blocks = exponents.shape[1]
    block_len = width // blocks
    scale = jnp.exp2(exponents.astype(jnp.float32))
    bf, f32 = jnp.bfloat16, jnp.float32
    vmem = pl.BlockSpec(memory_space=pltpu.VMEM)
    hbm = pl.BlockSpec(memory_space=pl.ANY)
    hops = n // 2
    dma = pltpu.SemaphoreType.DMA
    total = pl.pallas_call(
        functools.partial(kernel, n, length * n),
        out_shape=jax.ShapeDtypeStruct((rows, width), f32),
        in_specs=[vmem] * 5 + [hbm] * 4,
        out_specs=vmem,
        scratch_shapes=[
            pltpu.VMEM(queries.shape[1:], bf),
            pltpu.VMEM(targets.shape[1:], bf),
            pltpu.VMEM((rows, width), f32),
            pltpu.VMEM((rows, width), f32),
            pltpu.VMEM((rows, width), f32),
            pltpu.VMEM((steps, n, CHUNKS, rows, WIDE), bf),
            pltpu.VMEM((steps, n, CHUNKS, length, WIDE), bf),
            pltpu.VMEM((steps, n, length, rows), bf),
            pltpu.VMEM((steps, n, length, rows), bf),
            pltpu.VMEM((CHUNKS, length, WIDE), f32),
            pltpu.VMEM((CHUNKS, rows, WIDE), f32),
            pltpu.VMEM((2, CHUNKS, rows, WIDE), bf),
            dma((4,)),
            dma((steps, CHUNKS, 2, hops)),
            dma((steps, CHUNKS, 2, hops)),
            dma((steps, CHUNKS, 2, hops)),
            dma((steps, CHUNKS, 2, hops)),
            dma((steps, n)),
            dma((steps, n)),
            dma((CHUNKS,)),
            dma((CHUNKS,)),
        ],
        compiler_params=pltpu.CompilerParams(
            collective_id=0, has_side_effects=True, vmem_limit_bytes=60 * 2**20
        ),
    )(
        tokens[0], gain[None, :], base, offset[0], 1.0 / scale,
        queries[0], targets[0], first_moment[0], second_moment[0],
    )
    wide_scale = jnp.repeat(scale / replicas, block_len, axis=1)
    average = total * wide_scale
    new_momentum = 0.9 * outer_momentum + average
    new_base = base - 0.7 * (0.9 * new_momentum + average)
    return (new_base, new_momentum)


def solution(mesh):
    in_specs = (
        P(("job", "replica"), None, "fsdp", None),
        P(("job", "replica"), None, "fsdp", None),
        P(("job", "replica"), None, "fsdp", None),
        P(),
        P(("job", "fsdp"), None),
        P("replica", ("job", "fsdp"), None),
        P("replica", ("job", "fsdp"), None),
        P("replica", ("job", "fsdp"), None),
        P(("job", "fsdp"), None),
        P(("job", "fsdp"), None),
    )
    out_specs = (P(("job", "fsdp"), None), P(("job", "fsdp"), None))
    body = functools.partial(shards, mesh.shape["fsdp"], mesh.shape["replica"])
    return jax.shard_map(body, mesh=mesh, in_specs=in_specs, out_specs=out_specs, check_vma=False)
```

time: 377 us -> 175 us (0.46)
  waiting for transfers between devices: 234 us -> 0 us
  Pallas kernels: 0 us -> 168 us
  matrix products: 57 us -> 0 us
  blocking collectives: 29.1 us -> 0 us
  local copies, waits for them, and re-layouts: 19.1 us -> 1.47 us
  other arithmetic: 18.2 us -> 4.55 us
  between operations: 14.1 us -> 0.67 us
  starting transfers between devices: 4.63 us -> 0 us
    all_gather x4 -> x0, waiting for transfers between devices: 192 us -> none  [the longest x2 136 us: shards(): whole = lax.all_gather(wide, 'fsdp', axis=0, tiled=True)]
    pallas_call x0 -> x1, Pallas kernels: none -> 168 us  [shards(): pl.pallas_call(functools.partial(kernel, n, length * n), out_shape=jax.Sh...]
    dot_general x12 -> x0, matrix products: 46 us -> none  [the longest x2 16.6 us: sequence_grad(): jnp.einsum('hgqk,qhgd->khd', grad_sb, qh, preferred_element_type=jnp.floa...]
    all_to_all x1 -> x0, blocking collectives: 29.1 us -> none  [shards(): lax.all_to_all(normed, 'fsdp', split_axis=1, concat_axis=0, tiled=True)]
    all_to_all x1 -> x0, waiting for transfers between devices: 24.1 us -> none  [shards(): lax.all_to_all(normed, 'fsdp', split_axis=1, concat_axis=0, tiled=True)]
    psum x1 -> x0, waiting for transfers between devices: 17.4 us -> none  [shards(): lax.psum(coded.astype(jnp.float32).astype(jnp.bfloat16), 'replica')]
    convert_element_type x8 -> x0, other arithmetic: 11.3 us -> none  [the longest x2 4.04 us: shards(): wide = weights.astype(jnp.bfloat16)]
    sub x2 -> x0, matrix products: 11 us -> none  [sequence_grad(): expo = jnp.exp(scores - top)]
  transfers between devices with their start and end apart: 6 -> 0, of which waited for: 6 -> 0; matrix products, arithmetic and copies ran while one was open for 4% -> 0% of each run, Pallas kernels for 0% -> 0%
where the time goes in v1:
time: 175 us
  Pallas kernels  168 us (96%)
  other arithmetic  4.55 us (3%)
    pallas_call x1, Pallas kernels, shards(): pl.pallas_call(functools.partial(kernel, n, length * n), out_shape=jax.Sh...  168 us

profile of v1, /device:TPU:0, one launch (start us, length us, event | category | flops | bytes accessed | tf_op | source)
XLA Modules:
  0.0 175.1 jit_solution(17486551277768813344)
XLA Ops:
  0.6 0.7 broadcast_multiply_fusion
  1.3 0.1 copy.18
  1.5 0.1 copy.17
  1.6 0.7 broadcast_divide_fusion.inv_ref
  2.3 0.0 copy-start.1
  2.3 168.4 %shard_map.113 = f32[256,1024]{1,0:T(8,128)} custom-call(bf16[2,144,2048]{2,1,0:T(8,128)(2,1)} %bitcast.16, f32[1,2048]{1,0:T(1,128)} %bitcast.22, f32[256,1024]{1,0:T(8,128)} %base_ref.1, f32[256,1024]{1,0:T(8,128)} %bitcast.19, f32[256,8]{1,0:T(8,128)} %broadcast_divide_fusion.inv_ref, bf16[2,144,2048]{2,1,0:T(8,128)(2,1)} %bitcast.17, ...), custom_call_target="tpu_custom_call" | custom-call | tf_op jit(solution)/shard_map/pallas_call | solution.py:265
  170.7 0.0 copy-start
  170.7 0.3 broadcast_in_dim.7
  171.1 0.0 copy-done.1
  171.1 0.9 copy-done
  171.9 3.2 %multiply_subtract_fusion = (f32[256,1024]{1,0:T(8,128)}, f32[256,1024]{1,0:T(8,128)}) fusion(f32[256,1024]{1,0:T(8,128)S(1)} %copy-done, f32[256,1024]{1,0:T(8,128)} %shard_map.113, f32[32,8,8,128]{3,2,1,0:T(8,128)S(1)} %bitcast.15, f32[256,1024]{1,0:T(8,128)S(1)} %copy-done.1), kind=kLoop, calls=%fused_computation.1 | loop fusion | flops 1835008 | bytes 6291456 | tf_op jit(solution)/shard_map/sub | solution.py:303
Async XLA Ops:
  2.3 168.8 %copy-start.1 = (f32[256,1024]{1,0:T(8,128)S(1)}, f32[256,1024]{1,0:T(8,128)}, u32[]{:S(2)}) copy-start(f32[256,1024]{1,0:T(8,128)} %param.18) | copy-start | bytes 3145732
  170.7 1.2 copy-start
